TPU v7x, 32 devices: a whole 2x2x4 slice. The times are simulated.
32 devices in a mesh: wake: 16 (over z, y, core), col: 2 (over x).
Axes of the slice: x: 2, y: 2, z: 4, core: 2. Of those that a mesh axis runs over, the one named last changes fastest.
Arguments:
- points: float32 [3, 32768], P(None, ('wake', 'col')), may hold values from -6 to 6
- normals: float32 [3, 32768], P(None, ('wake', 'col')), may hold values from -6 to 6
- freestream: float32 [3], replicated, may hold values from -2 to 2
- wake_nodes: float32 [3, 16384], P(None, 'wake'), may hold values from -6 to 6
- circulation: float32 [16384], P('wake'), may hold values from -4 to 4
- filament: int32 [16384], P('wake'), may hold values from 0 to 127, never falling along the last dimension, each value on 1 to 256 neighbouring positions
- self_term: float32 [32768], P(('wake', 'col')), may hold values from 1 to 8
- near_blocks: float32 [256, 2, 1, 128, 128], P('wake', 'col'), may hold values from -0.5 to 0.5
- near_index: int32 [256, 2, 1], P('wake', 'col'), may hold values from 0 to 127
- far_left: float32 [2, 32, 32768], P('col', None, 'wake'), may hold values from -1 to 1
- far_right: float32 [16, 32, 32768], P('wake', None, 'col'), may hold values from -0.046875 to 0.046875
Outputs:
- right_side: float32 [32768], P(('wake', 'col'))
- strengths: float32 [32768], P(('wake', 'col'))
Inputs may be any that keep to these rules, and one draw needn't show every extreme that they name: Filament numbers never fall along the nodes; each filament has 1 to 256 nodes and one has exactly 256.
All inputs are finite; a program needn't handle non-finite values.
Results may differ from a plain program's by a relative error of at most 0.0004.
Values sent between devices are 32-bit elements; how exact they have to be, the bound alone decides.
No kernel may reach another device: no remote copies, remote signals or barrier semaphores. Data moves between devices by JAX's collectives and lax.ppermute only.
A program may use at most 64 MiB of HBM per device.

v0:
```python
import math
import jax
import jax.numpy as jnp
from jax import lax
from jax.sharding import PartitionSpec as P

KRYLOV = 6
core_sq = 0.01
four_pi = 4.0 * math.pi


def shifted(value, axis, steps):
    count = lax.axis_size(axis)
    first, last = (max(0, -steps), min(count, count - steps))
    return lax.ppermute(value, axis, [(source, source + steps) for source in range(first, last)])


def induce(points, normals, segments):
    near_arm = points[:, :, None] - segments[0:3, None, :]
    far_arm = points[:, :, None] - segments[3:6, None, :]
    cross_x = near_arm[1] * far_arm[2] - near_arm[2] * far_arm[1]
    cross_y = near_arm[2] * far_arm[0] - near_arm[0] * far_arm[2]
    cross_z = near_arm[0] * far_arm[1] - near_arm[1] * far_arm[0]
    normal_part = (
        cross_x * normals[0][:, None]
        + cross_y * normals[1][:, None]
        + cross_z * normals[2][:, None]
    )
    near_len = jnp.sqrt(jnp.sum(near_arm * near_arm, axis=0))
    far_len = jnp.sqrt(jnp.sum(far_arm * far_arm, axis=0))
    inner_dot = jnp.sum(near_arm * far_arm, axis=0)
    factor = (
        segments[6][None, :]
        * (near_len + far_len)
        / (four_pi * (near_len * far_len * (near_len * far_len + inner_dot) + core_sq))
    )
    return jnp.sum(factor * normal_part, axis=1)


def small_solve(gram_matrix, projected):
    size_now = gram_matrix.shape[0]
    factor = [[None for inner_pos in range(size_now)] for outer_pos in range(size_now)]
    for outer_pos in range(size_now):
        for inner_pos in range(outer_pos + 1):
            partial_sum = gram_matrix[outer_pos, inner_pos]
            for middle in range(inner_pos):
                partial_sum = partial_sum - factor[outer_pos][middle] * factor[inner_pos][middle]
            if inner_pos == outer_pos:
                factor[outer_pos][inner_pos] = jnp.sqrt(partial_sum)
            else:
                factor[outer_pos][inner_pos] = partial_sum / factor[inner_pos][inner_pos]
    forward = []
    for outer_pos in range(size_now):
        partial_sum = projected[outer_pos]
        for middle in range(outer_pos):
            partial_sum = partial_sum - factor[outer_pos][middle] * forward[middle]
        forward.append(partial_sum / factor[outer_pos][outer_pos])
    backward = [None for outer_pos in range(size_now)]
    for outer_pos in reversed(range(size_now)):
        partial_sum = forward[outer_pos]
        for middle in range(outer_pos + 1, size_now):
            partial_sum = partial_sum - factor[middle][outer_pos] * backward[middle]
        backward[outer_pos] = partial_sum / factor[outer_pos][outer_pos]
    return backward


def body(
    points,
    normals,
    freestream,
    wake_nodes,
    circulation,
    filament,
    self_term,
    near_blocks,
    near_index,
    far_left,
    far_right,
):
    highest = lax.Precision.HIGHEST
    piece_len = points.shape[1]
    filament_tag = filament.astype(jnp.float32) + 1.0
    first_node = jnp.concatenate([wake_nodes[:, 0], filament_tag[0:1]])
    following = shifted(first_node, "wake", -1)
    end_points = jnp.concatenate([wake_nodes[:, 1:], following[0:3, None]], axis=1)
    next_tag = jnp.concatenate([filament_tag[1:], following[3:4]])
    link_mask = (filament_tag == next_tag).astype(jnp.float32)
    segments = jnp.concatenate([wake_nodes, end_points, (circulation * link_mask)[None, :]], axis=0)
    shard_segs = lax.all_gather(segments, "wake", axis=1, tiled=True)
    seg_count = shard_segs.shape[1]
    add_block_len = math.gcd(seg_count, 512)

    def add_block(position, running):
        segment_block = lax.dynamic_slice_in_dim(
            shard_segs, position * add_block_len, add_block_len, 1
        )
        return running + induce(points, normals, segment_block)

    induced = lax.fori_loop(
        0, seg_count // add_block_len, add_block, jnp.zeros((piece_len,), jnp.float32)
    )
    right_side = -(jnp.dot(freestream, normals, precision=highest) + induced)
    block_len = near_blocks.shape[-1]
    local_blocks = near_blocks[:, 0]
    local_index = near_index[:, 0]
    left_factor = far_left[0]
    right_factor = far_right[0]
    initial_sq = lax.psum(jnp.sum(right_side * right_side), ("wake", "col"))
    initial_norm = jnp.sqrt(initial_sq)
    krylov = [right_side / initial_norm]
    hessenberg = jnp.zeros((KRYLOV + 1, KRYLOV), jnp.float32)
    for column in range(KRYLOV):
        vector = krylov[column]
        column_vec = lax.all_gather(vector, "wake", axis=0, tiled=True)
        far_coeff = jnp.dot(right_factor, column_vec, precision=highest)
        column_blocks = column_vec.reshape(-1, block_len)
        selected = column_blocks[local_index]
        near_part = jnp.einsum("rkij,rkj->ri", local_blocks, selected, precision=highest).reshape(
            piece_len * lax.axis_size("col")
        )
        summed = lax.psum_scatter(
            near_part + jnp.dot(far_coeff, left_factor, precision=highest),
            "col",
            scatter_dimension=0,
            tiled=True,
        )
        image_vec = self_term * vector + summed
        local_dots = jnp.stack([jnp.sum(image_vec * member) for member in krylov])
        coeffs = lax.psum(local_dots, ("wake", "col"))
        remainder = image_vec
        for position in range(column + 1):
            remainder = remainder - coeffs[position] * krylov[position]
        new_norm = jnp.sqrt(lax.psum(jnp.sum(remainder * remainder), ("wake", "col")))
        hessenberg = (
            hessenberg.at[: column + 1, column].set(coeffs).at[column + 1, column].set(new_norm)
        )
        if column + 1 < KRYLOV:
            krylov.append(remainder / new_norm)
    gram_matrix = jnp.dot(hessenberg.T, hessenberg, precision=highest)
    combination = small_solve(gram_matrix, initial_norm * hessenberg[0])
    strengths = combination[0] * krylov[0]
    for position in range(1, KRYLOV):
        strengths = strengths + combination[position] * krylov[position]
    return (right_side, strengths)


def solution(mesh):
    in_specs = (
        P(None, ("wake", "col")),
        P(None, ("wake", "col")),
        P(),
        P(None, "wake"),
        P("wake"),
        P("wake"),
        P(("wake", "col")),
        P("wake", "col", None, None, None),
        P("wake", "col", None),
        P("col", None, "wake"),
        P("wake", None, "col"),
    )
    out_specs = (P(("wake", "col")), P(("wake", "col")))
    return jax.shard_map(body, mesh=mesh, in_specs=in_specs, out_specs=out_specs, check_vma=False)
```

profile of v0, /device:TPU:0, one launch (start us, length us, event | category | flops | bytes accessed | tf_op | source)
XLA Modules:
  0.0 1426.7 jit_solution(15136460085953510115)
XLA Ops:
  18.1 26.6 %all_gather.21 = f32[7,16384]{1,0:T(8,128)} all-gather(f32[7,1024]{1,0:T(8,128)S(1)} %pad_maximum_fusion), channel_id=1, replica_groups=mesh['wake'=16,'col'=2] {'wake'}, dimensions={1}, use_global_device_ids=true | all-gather | bytes 487424 | tf_op jit(solution)/shard_map/all_gather | solution.py:89
  44.7 603.5 %while.26 = (s32[]{:T(128)}, f32[1024]{0:T(1024)S(1)}, f32[7,16384]{1,0:T(8,128)}, f32[3,1024]{1,0:T(4,128)}, f32[3,1024]{1,0:T(4,128)}, /*index=5*/s32[]{:T(128...) while((s32[]{:T(128)}, f32[1024]{0:T(1024)S(1)}, f32[7,16384]{1,0:T(8,128)}, ...), condition=%wide.region_5.0_spmd.clone, body=%wide.region_0.0_spmd.clone.sunk | while | flops 23593992 | bytes 37906656 | solution.py:99
  45.6 9.2 multiply_reduce_fusion.32
  55.6 7.9 fusion.107
  64.4 9.2 multiply_reduce_fusion.32
  74.4 7.9 fusion.107
  83.3 9.2 multiply_reduce_fusion.32
  102.1 9.2 multiply_reduce_fusion.32
  112.2 7.9 fusion.107
  121.0 9.2 multiply_reduce_fusion.32
  139.9 9.2 multiply_reduce_fusion.32
  158.7 9.2 multiply_reduce_fusion.32
  177.6 9.2 multiply_reduce_fusion.32
  196.4 9.2 multiply_reduce_fusion.32
  206.5 7.9 fusion.107
  215.3 9.2 multiply_reduce_fusion.32
  234.2 9.2 multiply_reduce_fusion.32
  253.0 9.2 multiply_reduce_fusion.32
  263.0 7.9 fusion.107
  271.9 9.2 multiply_reduce_fusion.32
  290.7 9.2 multiply_reduce_fusion.32
  309.6 9.2 multiply_reduce_fusion.32
  319.6 7.9 fusion.107
  328.5 9.2 multiply_reduce_fusion.32
  347.3 9.2 multiply_reduce_fusion.32
  357.3 7.9 fusion.107
  366.2 9.2 multiply_reduce_fusion.32
  385.0 9.2 multiply_reduce_fusion.32
  403.9 9.2 multiply_reduce_fusion.32
  413.9 7.9 fusion.107
  422.7 9.2 multiply_reduce_fusion.32
  441.6 9.2 multiply_reduce_fusion.32
  460.5 9.2 multiply_reduce_fusion.32
  470.5 7.9 fusion.107
  479.3 9.2 multiply_reduce_fusion.32
  498.2 9.2 multiply_reduce_fusion.32
  517.0 9.2 multiply_reduce_fusion.32
  535.9 9.2 multiply_reduce_fusion.32
  554.8 9.2 multiply_reduce_fusion.32
  564.8 7.9 fusion.107
  573.6 9.2 multiply_reduce_fusion.32
  592.5 9.2 multiply_reduce_fusion.32
  611.3 9.2 multiply_reduce_fusion.32
  621.4 7.9 fusion.107
  630.2 9.2 multiply_reduce_fusion.32
  649.3 37.1 %psum.91 = f32[]{:T(128)} all-reduce(f32[]{:T(128)} %multiply_reduce_fusion.30), channel_id=1, replica_groups=mesh['wake'=16,'col'=2] {'wake','col'}, use_global_device_ids=true, to_apply=%region_7.0 | all-reduce | flops 1 | bytes 8 | tf_op jit(solution)/shard_map/psum | solution.py:108
  687.8 21.4 %all_gather.22 = f32[16384]{0:T(1024)S(1)} all-gather(f32[1024]{0:T(1024)S(1)} %get-tuple-element.307), channel_id=1, replica_groups=mesh['wake'=16,'col'=2] {'wake'}, dimensions={0}, use_global_device_ids=true | all-gather | bytes 69632 | tf_op jit(solution)/shard_map/all_gather | solution.py:114
  719.1 37.1 %psum.92 = f32[1]{0:T(128)} all-reduce(f32[1]{0:T(128)} %bitcast.18), channel_id=1, replica_groups=mesh['wake'=16,'col'=2] {'wake','col'}, use_global_device_ids=true, to_apply=%region_10.0 | all-reduce | flops 1 | bytes 8 | tf_op jit(solution)/shard_map/psum | solution.py:129
  757.5 42.8 %psum.93 = f32[]{:T(128)} all-reduce(f32[]{:T(128)} %get-tuple-element.305), channel_id=1, replica_groups=mesh['wake'=16,'col'=2] {'wake','col'}, use_global_device_ids=true, to_apply=%region_12.0 | all-reduce | flops 1 | bytes 8 | tf_op jit(solution)/shard_map/psum | solution.py:133
  800.9 21.2 %all_gather.23 = f32[16384]{0:T(1024)S(1)} all-gather(f32[1024]{0:T(1024)S(1)} %broadcast_divide_fusion.4), channel_id=1, replica_groups=mesh['wake'=16,'col'=2] {'wake'}, dimensions={0}, use_global_device_ids=true | all-gather | bytes 69632 | tf_op jit(solution)/shard_map/all_gather | solution.py:114
  834.1 36.8 %psum.94 = f32[2]{0:T(128)S(1)} all-reduce(f32[2]{0:T(128)S(1)} %pad_maximum_fusion.2), channel_id=1, replica_groups=mesh['wake'=16,'col'=2] {'wake','col'}, use_global_device_ids=true, to_apply=%region_17.0 | all-reduce | flops 2 | bytes 16 | tf_op jit(solution)/shard_map/psum | solution.py:129
  873.4 41.5 %psum.95 = f32[]{:T(128)} all-reduce(f32[]{:T(128)} %get-tuple-element.302), channel_id=1, replica_groups=mesh['wake'=16,'col'=2] {'wake','col'}, use_global_device_ids=true, to_apply=%region_19.0 | all-reduce | flops 1 | bytes 8 | tf_op jit(solution)/shard_map/psum | solution.py:133
  915.7 20.8 %all_gather.24 = f32[16384]{0:T(1024)S(1)} all-gather(f32[1024]{0:T(1024)S(1)} %broadcast_divide_fusion.3), channel_id=1, replica_groups=mesh['wake'=16,'col'=2] {'wake'}, dimensions={0}, use_global_device_ids=true | all-gather | bytes 69632 | tf_op jit(solution)/shard_map/all_gather | solution.py:114
  948.4 36.9 %psum.96 = f32[3]{0:T(128)S(1)} all-reduce(f32[3]{0:T(128)S(1)} %pad_maximum_fusion.3), channel_id=1, replica_groups=mesh['wake'=16,'col'=2] {'wake','col'}, use_global_device_ids=true, to_apply=%region_25.0 | all-reduce | flops 3 | bytes 24 | tf_op jit(solution)/shard_map/psum | solution.py:129
  988.4 42.5 %psum.97 = f32[]{:T(128)} all-reduce(f32[]{:T(128)} %get-tuple-element.299), channel_id=1, replica_groups=mesh['wake'=16,'col'=2] {'wake','col'}, use_global_device_ids=true, to_apply=%region_27.0 | all-reduce | flops 1 | bytes 8 | tf_op jit(solution)/shard_map/psum | solution.py:133
  1031.5 20.9 %all_gather.25 = f32[16384]{0:T(1024)S(1)} all-gather(f32[1024]{0:T(1024)S(1)} %broadcast_divide_fusion.2), channel_id=1, replica_groups=mesh['wake'=16,'col'=2] {'wake'}, dimensions={0}, use_global_device_ids=true | all-gather | bytes 69632 | tf_op jit(solution)/shard_map/all_gather | solution.py:114
  1065.6 36.8 %psum.98 = f32[4]{0:T(128)S(1)} all-reduce(f32[4]{0:T(128)S(1)} %pad_maximum_fusion.4), channel_id=1, replica_groups=mesh['wake'=16,'col'=2] {'wake','col'}, use_global_device_ids=true, to_apply=%region_34.0 | all-reduce | flops 4 | bytes 32 | tf_op jit(solution)/shard_map/psum | solution.py:129
  1106.2 41.6 %psum.99 = f32[]{:T(128)} all-reduce(f32[]{:T(128)} %get-tuple-element.296), channel_id=1, replica_groups=mesh['wake'=16,'col'=2] {'wake','col'}, use_global_device_ids=true, to_apply=%region_36.0 | all-reduce | flops 1 | bytes 8 | tf_op jit(solution)/shard_map/psum | solution.py:133
  1148.5 20.8 %all_gather.26 = f32[16384]{0:T(1024)S(1)} all-gather(f32[1024]{0:T(1024)S(1)} %broadcast_divide_fusion.1), channel_id=1, replica_groups=mesh['wake'=16,'col'=2] {'wake'}, dimensions={0}, use_global_device_ids=true | all-gather | bytes 69632 | tf_op jit(solution)/shard_map/all_gather | solution.py:114
  1182.4 36.8 %psum.100 = f32[5]{0:T(128)S(1)} all-reduce(f32[5]{0:T(128)S(1)} %stack.96), channel_id=1, replica_groups=mesh['wake'=16,'col'=2] {'wake','col'}, use_global_device_ids=true, to_apply=%region_44.0 | all-reduce | flops 5 | bytes 40 | tf_op jit(solution)/shard_map/psum | solution.py:129
  1223.7 42.4 %psum.101 = f32[]{:T(128)} all-reduce(f32[]{:T(128)} %get-tuple-element.293), channel_id=1, replica_groups=mesh['wake'=16,'col'=2] {'wake','col'}, use_global_device_ids=true, to_apply=%region_46.0 | all-reduce | flops 1 | bytes 8 | tf_op jit(solution)/shard_map/psum | solution.py:133
  1266.8 20.9 %all_gather.27 = f32[16384]{0:T(1024)S(1)} all-gather(f32[1024]{0:T(1024)S(1)} %broadcast_divide_fusion), channel_id=1, replica_groups=mesh['wake'=16,'col'=2] {'wake'}, dimensions={0}, use_global_device_ids=true | all-gather | bytes 69632 | tf_op jit(solution)/shard_map/all_gather | solution.py:114
  1302.2 36.8 %psum.102 = f32[6]{0:T(128)S(1)} all-reduce(f32[6]{0:T(128)S(1)} %stack.103), channel_id=1, replica_groups=mesh['wake'=16,'col'=2] {'wake','col'}, use_global_device_ids=true, to_apply=%region_55.0 | all-reduce | flops 6 | bytes 48 | tf_op jit(solution)/shard_map/psum | solution.py:129
  1344.8 41.6 %psum.103 = f32[]{:T(128)} all-reduce(f32[]{:T(128)} %multiply_reduce_fusion.3), channel_id=1, replica_groups=mesh['wake'=16,'col'=2] {'wake','col'}, use_global_device_ids=true, to_apply=%region_57.0 | all-reduce | flops 1 | bytes 8 | tf_op jit(solution)/shard_map/psum | solution.py:133
  (342 shorter events, 355.6 us)
Async XLA Ops:
  0.6 710.9 %copy-start = (f32[1,32,16384]{2,1,0:T(8,128)S(1)}, f32[1,32,16384]{2,1,0:T(8,128)}, u32[]{:S(2)}) copy-start(f32[1,32,16384]{2,1,0:T(8,128)} %param.47) | copy-start | bytes 6291460
  3.5 11.7 collective-permute-start
  44.7 665.1 %copy-start.1 = (f32[16,1,1,128,128]{4,3,2,1,0:T(8,128)S(1)}, f32[16,1,1,128,128]{4,3,2,1,0:T(8,128)}, u32[]{:S(2)}) copy-start(f32[16,1,1,128,128]{4,3,2,1,0:T(8,128)} %param.44) | copy-start | bytes 3145732
  45.6 10.0 copy-start.3
  64.4 10.0 copy-start.3
  83.3 10.0 copy-start.3
  102.1 10.0 copy-start.3
  121.0 10.0 copy-start.3
  139.9 10.0 copy-start.3
  158.7 10.0 copy-start.3
  177.6 10.0 copy-start.3
  196.4 10.0 copy-start.3
  215.3 10.0 copy-start.3
  234.2 10.0 copy-start.3
  253.0 10.0 copy-start.3
  271.9 10.0 copy-start.3
  290.7 10.0 copy-start.3
  309.6 10.0 copy-start.3
  328.4 10.0 copy-start.3
  347.3 10.0 copy-start.3
  366.2 10.0 copy-start.3
  385.0 10.0 copy-start.3
  403.9 10.0 copy-start.3
  422.7 10.0 copy-start.3
  441.6 10.0 copy-start.3
  460.5 10.0 copy-start.3
  479.3 10.0 copy-start.3
  498.2 10.0 copy-start.3
  517.0 10.0 copy-start.3
  535.9 10.0 copy-start.3
  554.8 10.0 copy-start.3
  573.6 10.0 copy-start.3
  592.5 10.0 copy-start.3
  611.3 10.0 copy-start.3
  630.2 10.0 copy-start.3
  648.2 65.1 %copy-start.2 = (f32[1,32,2048]{2,1,0:T(8,128)S(1)}, f32[1,32,2048]{2,1,0:T(8,128)}, u32[]{:S(2)}) copy-start(f32[1,32,2048]{2,1,0:T(8,128)} %param.46) | copy-start | bytes 786436
  648.2 70.4 %copy-start.4 = (f32[1024]{0:T(1024)S(1)}, f32[1024]{0:T(1024)}, u32[]{:S(2)}) copy-start(f32[1024]{0:T(1024)} %param.43) | copy-start | bytes 12292
where the time goes:
time: 1450 us; the launch traced here: 1430 us
  blocking collectives  693 us (48%)
  other arithmetic  598 us (41%)
  local copies, waits for them, and re-layouts  85.1 us (6%)
  between operations  24.4 us (2%)
  matrix products  23.4 us (2%)
    reduce_sum x32, other arithmetic, induce(): near_len = jnp.sqrt(jnp.sum(near_arm * near_arm, axis=0))  295 us
    reduce_sum x32, other arithmetic, induce(): return jnp.sum(factor * normal_part, axis=1)  253 us
    psum x6, blocking collectives, body(): lax.psum(jnp.sum(remainder * remainder), ('wake', 'col'))  252 us
    psum x6, blocking collectives, body(): coeffs = lax.psum(local_dots, ('wake', 'col'))  221 us
    all_gather x6, blocking collectives, body(): column_vec = lax.all_gather(vector, 'wake', axis=0, tiled=True)  126 us
    psum x1, blocking collectives, body(): initial_sq = lax.psum(jnp.sum(right_side * right_side), ('wake', 'col'))  37.1 us
    unnamed x6, blocking collectives  30.1 us
  transfers between devices with their start and end apart: 1, of which 0 were waited for; matrix products, arithmetic and copies ran while one was open for 1% of the time, Pallas kernels for 0%

commit v1 on v0

--- a/solution.py
+++ b/solution.py
@@ -126,7 +126,9 @@
         )
         image_vec = self_term * vector + summed
         local_dots = jnp.stack([jnp.sum(image_vec * member) for member in krylov])
-        coeffs = lax.psum(local_dots, ("wake", "col"))
+        coeffs = local_dots
+        for j in ("col", "wake"):
+            coeffs = lax.psum(coeffs, j)
         remainder = image_vec
         for position in range(column + 1):
             remainder = remainder - coeffs[position] * krylov[position]

time: 1450 us -> 1400 us (0.966)
  blocking collectives: 693 us -> 653 us
    psum x6, blocking collectives: 252 us -> 222 us  [body(): lax.psum(jnp.sum(remainder * remainder), ('wake', 'col'))]
    psum x6 -> x12, blocking collectives: 221 us -> 208 us  [body(): coeffs = lax.psum(coeffs, j)]
  transfers between devices with their start and end apart: 1 -> 1, of which waited for: 0 -> 0; matrix products, arithmetic and copies ran while one was open for 1% -> 0% of each run, Pallas kernels for 0% -> 0%
where the time goes in v1:
time: 1400 us; the launch traced here: 1380 us
  blocking collectives  653 us (47%)
  other arithmetic  596 us (43%)
  local copies, waits for them, and re-layouts  85 us (6%)
  between operations  24.4 us (2%)
  matrix products  23.4 us (2%)
    reduce_sum x32, other arithmetic, induce(): near_len = jnp.sqrt(jnp.sum(near_arm * near_arm, axis=0))  295 us
    reduce_sum x32, other arithmetic, induce(): return jnp.sum(factor * normal_part, axis=1)  253 us
    psum x6, blocking collectives, body(): lax.psum(jnp.sum(remainder * remainder), ('wake', 'col'))  222 us
    psum x12, blocking collectives, body(): coeffs = lax.psum(coeffs, j)  208 us
    all_gather x6, blocking collectives, body(): column_vec = lax.all_gather(vector, 'wake', axis=0, tiled=True)  129 us
    psum x1, blocking collectives, body(): initial_sq = lax.psum(jnp.sum(right_side * right_side), ('wake', 'col'))  37.1 us
    unnamed x6, blocking collectives  30.1 us
  transfers between devices with their start and end apart: 1, of which 0 were waited for; matrix products, arithmetic and copies ran while one was open for 0% of the time, Pallas kernels for 0%

profile of v1, /device:TPU:0, one launch (start us, length us, event | category | flops | bytes accessed | tf_op | source)
XLA Modules:
  0.0 1383.9 jit_solution(15476005207193162302)
XLA Ops:
  14.1 26.6 %all_gather.21 = f32[7,16384]{1,0:T(8,128)} all-gather(f32[7,1024]{1,0:T(8,128)S(1)} %pad_maximum_fusion), channel_id=1, replica_groups=mesh['wake'=16,'col'=2] {'wake'}, dimensions={1}, use_global_device_ids=true | all-gather | bytes 487424 | tf_op jit(solution)/shard_map/all_gather | solution.py:89
  40.7 603.5 %while.26 = (s32[]{:T(128)}, f32[1024]{0:T(1024)S(1)}, f32[7,16384]{1,0:T(8,128)}, f32[3,1024]{1,0:T(4,128)}, f32[3,1024]{1,0:T(4,128)}, /*index=5*/s32[]{:T(128...) while((s32[]{:T(128)}, f32[1024]{0:T(1024)S(1)}, f32[7,16384]{1,0:T(8,128)}, ...), condition=%wide.region_5.0_spmd.clone, body=%wide.region_0.0_spmd.clone.sunk | while | flops 23593992 | bytes 37906656 | solution.py:99
  41.6 9.2 multiply_reduce_fusion.32
  51.6 7.9 fusion.107
  60.5 9.2 multiply_reduce_fusion.32
  79.3 9.2 multiply_reduce_fusion.32
  89.3 7.9 fusion.107
  98.2 9.2 multiply_reduce_fusion.32
  117.0 9.2 multiply_reduce_fusion.32
  135.9 9.2 multiply_reduce_fusion.32
  145.9 7.9 fusion.107
  154.8 9.2 multiply_reduce_fusion.32
  173.6 9.2 multiply_reduce_fusion.32
  192.5 9.2 multiply_reduce_fusion.32
  202.5 7.9 fusion.107
  211.3 9.2 multiply_reduce_fusion.32
  230.2 9.2 multiply_reduce_fusion.32
  240.2 7.9 fusion.107
  249.1 9.2 multiply_reduce_fusion.32
  267.9 9.2 multiply_reduce_fusion.32
  286.8 9.2 multiply_reduce_fusion.32
  296.8 7.9 fusion.107
  305.6 9.2 multiply_reduce_fusion.32
  324.5 9.2 multiply_reduce_fusion.32
  343.3 9.2 multiply_reduce_fusion.32
  353.4 7.9 fusion.107
  362.2 9.2 multiply_reduce_fusion.32
  381.1 9.2 multiply_reduce_fusion.32
  399.9 9.2 multiply_reduce_fusion.32
  418.8 9.2 multiply_reduce_fusion.32
  437.6 9.2 multiply_reduce_fusion.32
  447.7 7.9 fusion.107
  456.5 9.2 multiply_reduce_fusion.32
  475.4 9.2 multiply_reduce_fusion.32
  494.2 9.2 multiply_reduce_fusion.32
  504.2 7.9 fusion.107
  513.1 9.2 multiply_reduce_fusion.32
  531.9 9.2 multiply_reduce_fusion.32
  550.8 9.2 multiply_reduce_fusion.32
  560.8 7.9 fusion.107
  569.7 9.2 multiply_reduce_fusion.32
  588.5 9.2 multiply_reduce_fusion.32
  598.5 7.9 fusion.107
  607.4 9.2 multiply_reduce_fusion.32
  626.2 9.2 multiply_reduce_fusion.32
  645.5 37.1 %psum.133 = f32[]{:T(128)} all-reduce(f32[]{:T(128)} %multiply_reduce_fusion.30), channel_id=1, replica_groups=mesh['wake'=16,'col'=2] {'wake','col'}, use_global_device_ids=true, to_apply=%region_7.0 | all-reduce | flops 1 | bytes 8 | tf_op jit(solution)/shard_map/psum | solution.py:108
  683.9 21.4 %all_gather.22 = f32[16384]{0:T(1024)S(1)} all-gather(f32[1024]{0:T(1024)S(1)} %get-tuple-element.307), channel_id=1, replica_groups=mesh['wake'=16,'col'=2] {'wake'}, dimensions={0}, use_global_device_ids=true | all-gather | bytes 69632 | tf_op jit(solution)/shard_map/all_gather | solution.py:114
  721.6 30.1 %psum.135 = f32[1]{0:T(128)} all-reduce(f32[1]{0:T(128)} %psum.134), channel_id=1, replica_groups=mesh['wake'=16,'col'=2] {'wake'}, use_global_device_ids=true, to_apply=%region_11.0 | all-reduce | flops 1 | bytes 8 | tf_op jit(solution)/shard_map/psum | solution.py:131
  752.9 37.0 %psum.136 = f32[]{:T(128)} all-reduce(f32[]{:T(128)} %get-tuple-element.305), channel_id=1, replica_groups=mesh['wake'=16,'col'=2] {'wake','col'}, use_global_device_ids=true, to_apply=%region_13.0 | all-reduce | flops 1 | bytes 8 | tf_op jit(solution)/shard_map/psum | solution.py:135
  790.6 21.6 %all_gather.23 = f32[16384]{0:T(1024)S(1)} all-gather(f32[1024]{0:T(1024)S(1)} %broadcast_divide_fusion.4), channel_id=1, replica_groups=mesh['wake'=16,'col'=2] {'wake'}, dimensions={0}, use_global_device_ids=true | all-gather | bytes 69632 | tf_op jit(solution)/shard_map/all_gather | solution.py:114
  829.6 29.5 %psum.138 = f32[2]{0:T(128)S(1)} all-reduce(f32[2]{0:T(128)S(1)} %psum.137), channel_id=1, replica_groups=mesh['wake'=16,'col'=2] {'wake'}, use_global_device_ids=true, to_apply=%region_19.0 | all-reduce | flops 2 | bytes 16 | tf_op jit(solution)/shard_map/psum | solution.py:131
  861.4 37.1 %psum.139 = f32[]{:T(128)} all-reduce(f32[]{:T(128)} %get-tuple-element.302), channel_id=1, replica_groups=mesh['wake'=16,'col'=2] {'wake','col'}, use_global_device_ids=true, to_apply=%region_21.0 | all-reduce | flops 1 | bytes 8 | tf_op jit(solution)/shard_map/psum | solution.py:135
  899.2 21.5 %all_gather.24 = f32[16384]{0:T(1024)S(1)} all-gather(f32[1024]{0:T(1024)S(1)} %broadcast_divide_fusion.3), channel_id=1, replica_groups=mesh['wake'=16,'col'=2] {'wake'}, dimensions={0}, use_global_device_ids=true | all-gather | bytes 69632 | tf_op jit(solution)/shard_map/all_gather | solution.py:114
  938.0 29.5 %psum.141 = f32[3]{0:T(128)S(1)} all-reduce(f32[3]{0:T(128)S(1)} %psum.140), channel_id=1, replica_groups=mesh['wake'=16,'col'=2] {'wake'}, use_global_device_ids=true, to_apply=%region_28.0 | all-reduce | flops 3 | bytes 24 | tf_op jit(solution)/shard_map/psum | solution.py:131
  970.7 37.0 %psum.142 = f32[]{:T(128)} all-reduce(f32[]{:T(128)} %get-tuple-element.299), channel_id=1, replica_groups=mesh['wake'=16,'col'=2] {'wake','col'}, use_global_device_ids=true, to_apply=%region_30.0 | all-reduce | flops 1 | bytes 8 | tf_op jit(solution)/shard_map/psum | solution.py:135
  1008.4 21.5 %all_gather.25 = f32[16384]{0:T(1024)S(1)} all-gather(f32[1024]{0:T(1024)S(1)} %broadcast_divide_fusion.2), channel_id=1, replica_groups=mesh['wake'=16,'col'=2] {'wake'}, dimensions={0}, use_global_device_ids=true | all-gather | bytes 69632 | tf_op jit(solution)/shard_map/all_gather | solution.py:114
  1048.0 29.7 %psum.144 = f32[4]{0:T(128)S(1)} all-reduce(f32[4]{0:T(128)S(1)} %psum.143), channel_id=1, replica_groups=mesh['wake'=16,'col'=2] {'wake'}, use_global_device_ids=true, to_apply=%region_38.0 | all-reduce | flops 4 | bytes 32 | tf_op jit(solution)/shard_map/psum | solution.py:131
  1081.5 37.0 %psum.145 = f32[]{:T(128)} all-reduce(f32[]{:T(128)} %get-tuple-element.296), channel_id=1, replica_groups=mesh['wake'=16,'col'=2] {'wake','col'}, use_global_device_ids=true, to_apply=%region_40.0 | all-reduce | flops 1 | bytes 8 | tf_op jit(solution)/shard_map/psum | solution.py:135
  1119.2 21.5 %all_gather.26 = f32[16384]{0:T(1024)S(1)} all-gather(f32[1024]{0:T(1024)S(1)} %broadcast_divide_fusion.1), channel_id=1, replica_groups=mesh['wake'=16,'col'=2] {'wake'}, dimensions={0}, use_global_device_ids=true | all-gather | bytes 69632 | tf_op jit(solution)/shard_map/all_gather | solution.py:114
  1159.4 29.5 %psum.147 = f32[5]{0:T(128)S(1)} all-reduce(f32[5]{0:T(128)S(1)} %psum.146), channel_id=1, replica_groups=mesh['wake'=16,'col'=2] {'wake'}, use_global_device_ids=true, to_apply=%region_49.0 | all-reduce | flops 5 | bytes 40 | tf_op jit(solution)/shard_map/psum | solution.py:131
  1193.3 37.1 %psum.148 = f32[]{:T(128)} all-reduce(f32[]{:T(128)} %get-tuple-element.293), channel_id=1, replica_groups=mesh['wake'=16,'col'=2] {'wake','col'}, use_global_device_ids=true, to_apply=%region_51.0 | all-reduce | flops 1 | bytes 8 | tf_op jit(solution)/shard_map/psum | solution.py:135
  1231.0 21.5 %all_gather.27 = f32[16384]{0:T(1024)S(1)} all-gather(f32[1024]{0:T(1024)S(1)} %broadcast_divide_fusion), channel_id=1, replica_groups=mesh['wake'=16,'col'=2] {'wake'}, dimensions={0}, use_global_device_ids=true | all-gather | bytes 69632 | tf_op jit(solution)/shard_map/all_gather | solution.py:114
  1271.8 29.5 %psum.150 = f32[6]{0:T(128)S(1)} all-reduce(f32[6]{0:T(128)S(1)} %psum.149), channel_id=1, replica_groups=mesh['wake'=16,'col'=2] {'wake'}, use_global_device_ids=true, to_apply=%region_61.0 | all-reduce | flops 6 | bytes 48 | tf_op jit(solution)/shard_map/psum | solution.py:131
  1306.9 37.1 %psum.151 = f32[]{:T(128)} all-reduce(f32[]{:T(128)} %multiply_reduce_fusion.3), channel_id=1, replica_groups=mesh['wake'=16,'col'=2] {'wake','col'}, use_global_device_ids=true, to_apply=%region_63.0 | all-reduce | flops 1 | bytes 8 | tf_op jit(solution)/shard_map/psum | solution.py:135
  (352 shorter events, 383.6 us)
Async XLA Ops:
  0.6 707.0 %copy-start = (f32[1,32,16384]{2,1,0:T(8,128)S(1)}, f32[1,32,16384]{2,1,0:T(8,128)}, u32[]{:S(2)}) copy-start(f32[1,32,16384]{2,1,0:T(8,128)} %param.47) | copy-start | bytes 6291460
  3.5 7.7 collective-permute-start
  40.7 665.2 %copy-start.1 = (f32[16,1,1,128,128]{4,3,2,1,0:T(8,128)S(1)}, f32[16,1,1,128,128]{4,3,2,1,0:T(8,128)}, u32[]{:S(2)}) copy-start(f32[16,1,1,128,128]{4,3,2,1,0:T(8,128)} %param.44) | copy-start | bytes 3145732
  41.6 10.0 copy-start.3
  60.5 10.0 copy-start.3
  79.3 10.0 copy-start.3
  98.2 10.0 copy-start.3
  117.0 10.0 copy-start.3
  135.9 10.0 copy-start.3
  154.8 10.0 copy-start.3
  173.6 10.0 copy-start.3
  192.5 10.0 copy-start.3
  211.3 10.0 copy-start.3
  230.2 10.0 copy-start.3
  249.0 10.0 copy-start.3
  267.9 10.0 copy-start.3
  286.8 10.0 copy-start.3
  305.6 10.0 copy-start.3
  324.5 10.0 copy-start.3
  343.3 10.0 copy-start.3
  362.2 10.0 copy-start.3
  381.1 10.0 copy-start.3
  399.9 10.0 copy-start.3
  418.8 10.0 copy-start.3
  437.6 10.0 copy-start.3
  456.5 10.0 copy-start.3
  475.4 10.0 copy-start.3
  494.2 10.0 copy-start.3
  513.1 10.0 copy-start.3
  531.9 10.0 copy-start.3
  550.8 10.0 copy-start.3
  569.7 10.0 copy-start.3
  588.5 10.0 copy-start.3
  607.4 10.0 copy-start.3
  626.2 10.0 copy-start.3
  644.2 65.2 %copy-start.2 = (f32[1,32,2048]{2,1,0:T(8,128)S(1)}, f32[1,32,2048]{2,1,0:T(8,128)}, u32[]{:S(2)}) copy-start(f32[1,32,2048]{2,1,0:T(8,128)} %param.46) | copy-start | bytes 786436
  644.2 70.5 %copy-start.4 = (f32[1024]{0:T(1024)S(1)}, f32[1024]{0:T(1024)}, u32[]{:S(2)}) copy-start(f32[1024]{0:T(1024)} %param.43) | copy-start | bytes 12292
  644.2 76.6 %copy-start.6 = (s32[2]{0:T(128)S(1)}, s32[2]{0:T(128)}, u32[]{:S(2)}) copy-start(s32[2]{0:T(128)} %constant.361.clone.1) | copy-start | bytes 28
  709.4 114.0 %copy-start.5 = (s32[2]{0:T(128)S(1)}, s32[2]{0:T(128)}, u32[]{:S(2)}) copy-start(s32[2]{0:T(128)} %constant.362.clone.1) | copy-start | bytes 28
